TPU v7x, 32 devices: a whole 2x2x4 slice. The times are simulated.
32 devices in a mesh: group: 4 (over y, core), inner: 8 (over z, x).
Axes of the slice: x: 2, y: 2, z: 4, core: 2. Of those that a mesh axis runs over, the one named last changes fastest.
Arguments:
- left_part: bfloat16 [32768, 256], P(('group', 'inner')), may hold values from -12 to 12
- right_part: bfloat16 [32768, 256], P(('group', 'inner')), may hold values from -12 to 12
- relation: bfloat16 [256, 256], replicated, may hold values from -0.19 to 1.19
- src_index: int32 [32, 4, 512], P(('group', 'inner')), may hold values from 0 to 1023
- dst_index: int32 [32, 4, 512], P(('group', 'inner')), may hold values from 0 to 1023
- lengths: int32 [32, 4], P(('group', 'inner')), may hold values from 1 to 512, 1280 in all within a row
Outputs:
- left_out: bfloat16 [32768, 256], P(('group', 'inner'))
- right_out: bfloat16 [32768, 256], P(('group', 'inner'))
- relation_out: float32 [256, 256], replicated
All inputs are finite; a program needn't handle non-finite values.
Results may differ from a plain program's by a relative error of at most 0.012.
The roundings to bfloat16 on the way count: a program that leaves them out, or rounds other values in their place, can miss the bound.
Values may be sent and summed in bfloat16 or wider, within the bound.
A program may use at most 64 MiB of HBM per device.

v0:
```python
import jax
import jax.numpy as jnp
from jax import lax
from jax.sharding import PartitionSpec as P

MEETINGS = 4


SCORE_SCALE = 0.1875
LR_EMBED = 0.5
LR_RELATION = 0.02


def swapped(value, axis, distance):
    mask = 2**distance
    pairs = [(source, source ^ mask) for source in range(lax.axis_size(axis))]
    return lax.ppermute(value, axis, pairs)


def bucket(left_block, holding, relation, src_row, dst_row, length):
    row_ids = jnp.arange(left_block.shape[0], dtype=jnp.int32)
    src_table = (src_row[:, None] == row_ids[None, :]).astype(jnp.bfloat16)
    picked = jnp.dot(src_table, left_block, preferred_element_type=jnp.float32).astype(jnp.bfloat16)
    queries = jnp.dot(picked, relation, preferred_element_type=jnp.float32).astype(jnp.bfloat16)
    scores = (
        lax.dot_general(
            queries, holding, (((1,), (1,)), ((), ())), preferred_element_type=jnp.float32
        )
        * SCORE_SCALE
    )
    maxima = jnp.max(scores, axis=1, keepdims=True)
    expos = jnp.exp(scores - maxima)
    softmax_w = expos / jnp.sum(expos, axis=1, keepdims=True)
    slot_ids = jnp.arange(src_row.shape[0], dtype=jnp.int32)
    live_mask = (slot_ids < length).astype(jnp.float32)
    columns = jnp.arange(holding.shape[0], dtype=jnp.int32)
    target = (columns[None, :] == dst_row[:, None]).astype(jnp.float32)
    coeffs = ((softmax_w - target) * live_mask[:, None]).astype(jnp.bfloat16)
    held_grad = (
        lax.dot_general(
            coeffs, queries, (((0,), (0,)), ((), ())), preferred_element_type=jnp.float32
        )
        * SCORE_SCALE
    )
    new_holding = (holding.astype(jnp.float32) - LR_EMBED * held_grad).astype(jnp.bfloat16)
    query_grad = (
        jnp.dot(coeffs, holding, preferred_element_type=jnp.float32) * SCORE_SCALE
    ).astype(jnp.bfloat16)
    relation_grad = lax.dot_general(
        picked, query_grad, (((0,), (0,)), ((), ())), preferred_element_type=jnp.float32
    )
    summed_rows = lax.dot_general(
        src_table, query_grad, (((0,), (0,)), ((), ())), preferred_element_type=jnp.float32
    )
    left_grad = lax.dot_general(
        summed_rows,
        relation.astype(jnp.float32),
        (((1,), (1,)), ((), ())),
        precision=lax.Precision.HIGHEST,
        preferred_element_type=jnp.float32,
    )
    new_left = (left_block.astype(jnp.float32) - LR_EMBED * left_grad).astype(jnp.bfloat16)
    return (new_left, new_holding, relation_grad)


def shards(left_part, right_part, relation, src_index, dst_index, lengths):
    log_inner = lax.axis_size("inner").bit_length() - 1
    left_block = left_part
    holding = right_part
    grad_total = jnp.zeros(relation.shape, jnp.float32)
    for meeting in range(MEETINGS):
        holding = swapped(holding, "inner", meeting % log_inner)
        left_block, holding, relation_grad = bucket(
            left_block,
            holding,
            relation,
            src_index[0, meeting],
            dst_index[0, meeting],
            lengths[0, meeting],
        )
        grad_total = grad_total + lax.psum(relation_grad, ("group", "inner"))
    relation_out = relation.astype(jnp.float32) - LR_RELATION * grad_total
    return (left_block, holding, relation_out)


def solution(mesh):
    in_specs = (
        P(("group", "inner"), None),
        P(("group", "inner"), None),
        P(),
        P(("group", "inner"), None, None),
        P(("group", "inner"), None, None),
        P(("group", "inner"), None),
    )
    out_specs = (P(("group", "inner"), None), P(("group", "inner"), None), P())
    return jax.shard_map(shards, mesh=mesh, in_specs=in_specs, out_specs=out_specs, check_vma=False)
```

profile of v0, /device:TPU:0, one launch (start us, length us, event | category | flops | bytes accessed | tf_op | source)
XLA Modules:
  0.0 219.8 jit_solution(11446270529863015966)
XLA Ops:
  7.2 3.0 %collective-permute-start = (bf16[1024,256]{1,0:T(8,128)(2,1)}, bf16[1024,256]{1,0:T(8,128)(2,1)S(1)}, u32[]{:S(2)}, u32[]{:S(2)}) collective-permute-start(bf16[1024,256]{1,0:T(8,128)(2,1)} %param.7), channel_id=1, source_target_pairs={{0,1},{1,0},{2,3},{3,2},{4,5},{5,4},{6,7},{7,6},{8,9},{9,8},{10,11... | collective-permute-start | bytes 1572872 | tf_op jit(solution)/shard_map/ppermute | solution.py:17
  10.2 1.5 fusion.42
  11.7 0.6 fusion.39
  12.3 0.7 fusion.37
  13.0 0.7 fusion.36
  13.7 0.9 fusion.41
  14.5 0.9 fusion.40
  15.4 0.7 fusion.38
  16.1 1.6 fusion.24
  17.6 1.1 convolution_convert_fusion.3
  18.8 3.6 %collective-permute-done = bf16[1024,256]{1,0:T(8,128)(2,1)S(1)} collective-permute-done((bf16[1024,256]{1,0:T(8,128)(2,1)}, bf16[1024,256]{1,0:T(8,128)(2,1)S(1)}, u32[]{:S(2)}, u32[]{:S(2)}) %collective-permute-start) | collective-permute-done | bytes 524320 | tf_op jit(solution)/shard_map/ppermute | solution.py:17
  22.3 0.6 multiply_reduce_fusion.3
  22.9 0.5 fusion.8
  23.4 0.8 multiply_convert_fusion.3
  24.2 0.5 subtract_convert_fusion.3
  24.8 1.9 collective-permute-start.1
  27.1 0.8 fusion.6
  27.9 0.6 fusion.16
  28.6 0.5 fusion.25
  29.6 8.3 %collective-permute-done.1 = bf16[1024,256]{1,0:T(8,128)(2,1)S(1)} collective-permute-done((bf16[1024,256]{1,0:T(8,128)(2,1)S(1)}, bf16[1024,256]{1,0:T(8,128)(2,1)S(1)}, u32[]{:S(2)}, u32[]{:S(2)}) %collective-permute-start.1) | collective-permute-done | bytes 524320 | tf_op jit(solution)/shard_map/ppermute | solution.py:17
  37.9 0.6 multiply_reduce_fusion.2
  38.5 0.5 fusion.9
  39.0 0.8 multiply_convert_fusion.2
  39.8 0.5 subtract_convert_fusion.2
  40.3 2.6 %collective-permute-start.2 = (bf16[1024,256]{1,0:T(8,128)(2,1)S(1)}, bf16[1024,256]{1,0:T(8,128)(2,1)S(1)}, u32[]{:S(2)}, u32[]{:S(2)}) collective-permute-start(bf16[1024,256]{1,0:T(8,128)(2,1)S(1)} %subtract_convert_fusion.2), channel_id=1, source_target_pairs={{0,4},{1,5},{2,6},{3,7},{4,0},{5,1},{6,2},{7,3},{8,12},{9,13},{10,... | collective-permute-start | bytes 1572872 | tf_op jit(solution)/shard_map/ppermute | solution.py:17
  43.4 0.8 fusion.4
  44.2 0.6 fusion.17
  44.8 0.5 fusion.26
  45.8 18.9 %collective-permute-done.2 = bf16[1024,256]{1,0:T(8,128)(2,1)S(1)} collective-permute-done((bf16[1024,256]{1,0:T(8,128)(2,1)S(1)}, bf16[1024,256]{1,0:T(8,128)(2,1)S(1)}, u32[]{:S(2)}, u32[]{:S(2)}) %collective-permute-start.2) | collective-permute-done | bytes 524320 | tf_op jit(solution)/shard_map/ppermute | solution.py:17
  64.7 0.6 multiply_reduce_fusion.1
  65.3 0.5 fusion.10
  65.8 1.0 multiply_convert_fusion.1
  66.8 0.5 subtract_convert_fusion.1
  67.3 1.2 collective-permute-start.3
  68.9 0.8 fusion.2
  69.7 0.6 fusion.18
  70.4 0.5 fusion.27
  71.4 9.1 %collective-permute-done.3 = bf16[1024,256]{1,0:T(8,128)(2,1)S(1)} collective-permute-done((bf16[1024,256]{1,0:T(8,128)(2,1)S(1)}, bf16[1024,256]{1,0:T(8,128)(2,1)S(1)}, u32[]{:S(2)}, u32[]{:S(2)}) %collective-permute-start.3) | collective-permute-done | bytes 524320 | tf_op jit(solution)/shard_map/ppermute | solution.py:17
  80.5 0.6 multiply_reduce_fusion
  81.0 0.5 fusion.11
  81.6 0.8 multiply_convert_fusion
  82.4 0.4 fusion.23
  82.8 0.8 fusion
  83.6 1.0 convolution_add_fusion
  84.6 1.3 subtract_convert_fusion
  85.9 1.4 fusion.19
  87.4 123.9 %all-reduce.2.cloned.1.call-done = f32[256,256]{1,0:T(8,128)} async-done(((f32[256,256]{1,0:T(8,128)}), f32[256,256]{1,0:T(8,128)}) %all-reduce.2.cloned.1.call-update) | async-done | bytes 262160 | tf_op jit(solution)/shard_map/psum | solution.py:81
  211.3 1.7 multiply_subtract_fusion
  (15 shorter events, 2.8 us)
Async XLA Ops:
  7.2 204.1 %all-reduce.2.cloned.1.call-start = ((), (), s32[]{:S(2)}) async-start(), calls=%async_computation | async-start | bytes 524288 | tf_op jit(solution)/shard_map/psum | solution.py:81
  7.2 15.1 %collective-permute-start = (bf16[1024,256]{1,0:T(8,128)(2,1)}, bf16[1024,256]{1,0:T(8,128)(2,1)S(1)}, u32[]{:S(2)}, u32[]{:S(2)}) collective-permute-start(bf16[1024,256]{1,0:T(8,128)(2,1)} %param.7), channel_id=1, source_target_pairs={{0,1},{1,0},{2,3},{3,2},{4,5},{5,4},{6,7},{7,6},{8,9},{9,8},{10,11... | collective-permute-start | bytes 1572872 | tf_op jit(solution)/shard_map/ppermute | solution.py:17
  24.7 3.2 %copy-start = (bf16[256,256]{1,0:T(8,128)(2,1)S(1)}, bf16[256,256]{1,0:T(8,128)(2,1)}, u32[]{:S(2)}) copy-start(bf16[256,256]{1,0:T(8,128)(2,1)} %param.8) | copy-start | bytes 393220
  24.7 3.2 %copy-start.1 = (bf16[1024,256]{1,0:T(8,128)(2,1)S(1)}, bf16[1024,256]{1,0:T(8,128)(2,1)}, u32[]{:S(2)}) copy-start(bf16[1024,256]{1,0:T(8,128)(2,1)} %param.6) | copy-start | bytes 1572868
  24.8 13.2 %collective-permute-start.1 = (bf16[1024,256]{1,0:T(8,128)(2,1)S(1)}, bf16[1024,256]{1,0:T(8,128)(2,1)S(1)}, u32[]{:S(2)}, u32[]{:S(2)}) collective-permute-start(bf16[1024,256]{1,0:T(8,128)(2,1)S(1)} %subtract_convert_fusion.3), channel_id=1, source_target_pairs={{0,2},{1,3},{2,0},{3,1},{4,6},{5,7},{6,4},{7,5},{8,10},{9,11},{10,... | collective-permute-start | bytes 1572872 | tf_op jit(solution)/shard_map/ppermute | solution.py:17
  40.3 24.4 %collective-permute-start.2 = (bf16[1024,256]{1,0:T(8,128)(2,1)S(1)}, bf16[1024,256]{1,0:T(8,128)(2,1)S(1)}, u32[]{:S(2)}, u32[]{:S(2)}) collective-permute-start(bf16[1024,256]{1,0:T(8,128)(2,1)S(1)} %subtract_convert_fusion.2), channel_id=1, source_target_pairs={{0,4},{1,5},{2,6},{3,7},{4,0},{5,1},{6,2},{7,3},{8,12},{9,13},{10,... | collective-permute-start | bytes 1572872 | tf_op jit(solution)/shard_map/ppermute | solution.py:17
  67.3 13.2 %collective-permute-start.3 = (bf16[1024,256]{1,0:T(8,128)(2,1)S(1)}, bf16[1024,256]{1,0:T(8,128)(2,1)S(1)}, u32[]{:S(2)}, u32[]{:S(2)}) collective-permute-start(bf16[1024,256]{1,0:T(8,128)(2,1)S(1)} %subtract_convert_fusion.1), channel_id=1, source_target_pairs={{0,1},{1,0},{2,3},{3,2},{4,5},{5,4},{6,7},{7,6},{8,9},{9,8},{10,11... | collective-permute-start | bytes 1572872 | tf_op jit(solution)/shard_map/ppermute | solution.py:17
Sparse Core Ops, SparseCore 0:
  84.8 126.5 all-reduce.1
where the time goes:
time: 220 us
  waiting for transfers between devices  164 us (75%)
  matrix products  20 us (9%)
  between operations  14.3 us (6%)
  other arithmetic  9.83 us (4%)
  starting transfers between devices  8.7 us (4%)
  local copies, waits for them, and re-layouts  3.2 us (1%)
    psum x1, waiting for transfers between devices, shards(): grad_total = grad_total + lax.psum(relation_grad, ('group', 'inner'))  124 us
    ppermute x4, waiting for transfers between devices, swapped(): return lax.ppermute(value, axis, pairs)  39.9 us
    ppermute x4, starting transfers between devices, swapped(): return lax.ppermute(value, axis, pairs)  8.66 us
  transfers between devices with their start and end apart: 5, of which 5 were waited for; matrix products, arithmetic and copies ran while one was open for 9% of the time, Pallas kernels for 0%

commit v1 on v0

v1 whole, which is shorter than its diff:
```python
import jax
import jax.numpy as jnp
from jax import lax
from jax.experimental import pallas as pl
from jax.experimental.pallas import tpu as pltpu
from jax.sharding import PartitionSpec as P

MEETINGS = 4

SCORE_SCALE = 0.1875
LR_EMBED = 0.5
LR_RELATION = 0.02

MESH = pl.DeviceIdType.MESH
F32 = jnp.float32
BF16 = jnp.bfloat16

ROW_CHUNKS = 4
EDGE_CHUNKS = 2


def partner(index, mask):
    return index + mask * (1 - 2 * lax.rem(lax.div(index, mask), 2))


def dot(a, b, a_dim, b_dim):
    return lax.dot_general(a, b, (((a_dim,), (b_dim,)), ((), ())), preferred_element_type=F32)


def kernel(
    n_inner,
    n_group,
    left_ref,
    right_ref,
    rel_ref,
    src_ref,
    dst_ref,
    len_ref,
    left_out,
    right_out,
    rel_out,
    met0,
    met1,
    met2,
    own2,
    next3,
    picked,
    query,
    query_in1,
    query_in2,
    grad_out1,
    grad_in1,
    coeffs,
    onehot,
    meta,
    meta_in1,
    meta_in3,
    part,
    part_in,
    shard,
    shard_in,
    gathered,
    move0_send,
    move0_recv,
    move2_send,
    move2_recv,
    move3_send,
    move3_recv,
    small_send,
    small_recv,
    rs_send,
    rs_recv,
    ar_send,
    ar_recv,
    ag_send,
    ag_recv,
):
    me = lax.axis_index("inner")
    my_group = lax.axis_index("group")
    rows, _ = left_ref.shape
    slots = src_ref.shape[2]
    log_inner = n_inner.bit_length() - 1
    masks = [2 ** (m % log_inner) for m in range(MEETINGS)]
    first = partner(me, masks[0])
    second = partner(me, masks[1])
    third = partner(second, masks[2])
    fourth = partner(me, masks[3])
    chunk = rows // ROW_CHUNKS
    width = slots // EDGE_CHUNKS

    def inner_id(index):
        return (my_group, index)

    def group_id(index):
        return (index, me)

    def remote(src, dst, send, recv, device):
        return pltpu.make_async_remote_copy(
            src_ref=src, dst_ref=dst, send_sem=send, recv_sem=recv, device_id=device, device_id_type=MESH
        )

    def piece(i):
        return pl.ds(i * chunk, chunk)

    barrier = pltpu.get_barrier_semaphore()
    for step in range(1, n_inner):
        pl.semaphore_signal(
            barrier, inc=1, device_id=inner_id(lax.rem(me + step, n_inner)), device_id_type=MESH
        )
    for step in range(1, n_group):
        pl.semaphore_signal(
            barrier, inc=1, device_id=group_id(lax.rem(my_group + step, n_group)), device_id_type=MESH
        )
    pl.semaphore_wait(barrier, n_inner + n_group - 2)

    move0 = [
        remote(right_ref.at[piece(i)], met0.at[piece(i)], move0_send.at[i], move0_recv.at[i], inner_id(first))
        for i in range(ROW_CHUNKS)
    ]
    for copy in move0:
        copy.start()

    slot_ids = lax.broadcasted_iota(jnp.int32, (1, slots), 1)
    meta[...] = jnp.zeros_like(meta)
    for m in range(MEETINGS):
        meta[m : m + 1, :] = jnp.where(slot_ids < len_ref[0:1, m : m + 1], dst_ref[0, m : m + 1, :], -1)
    meta1 = remote(meta, meta_in1, small_send.at[0], small_recv.at[0], inner_id(second))
    meta3 = remote(meta, meta_in3, small_send.at[1], small_recv.at[1], inner_id(fourth))
    meta1.start()
    meta3.start()

    entity = lax.broadcasted_iota(jnp.int32, (rows, width), 0)

    def columns(i):
        return slice(i * width, (i + 1) * width)

    def make_queries(m, table):
        for i in range(EDGE_CHUNKS):
            hot = (entity == src_ref[0, m : m + 1, columns(i)]).astype(F32).astype(BF16)
            onehot[:, columns(i)] = hot
            chosen = dot(table, hot, 0, 0).astype(BF16)
            picked[:, columns(i)] = chosen
            query[m, :, columns(i)] = dot(rel_ref[...], chosen, 0, 0).astype(BF16)

    def make_coeffs(holding, asked, targets):
        for i in range(EDGE_CHUNKS):
            scores = dot(holding, asked[:, columns(i)], 1, 0) * SCORE_SCALE
            expos = jnp.exp(scores - jnp.max(scores, axis=0, keepdims=True))
            weight = expos * (1.0 / jnp.sum(expos, axis=0, keepdims=True))
            target = targets[:, columns(i)]
            weight = weight - (entity == target).astype(F32)
            weight = weight * (target >= 0).astype(F32)
            coeffs[:, columns(i)] = weight.astype(BF16)

    def query_grad(holding):
        return (dot(holding, coeffs[...], 0, 0) * SCORE_SCALE).astype(BF16)

    def held_update(holding, asked, i):
        held_grad = dot(coeffs[piece(i), :], asked, 1, 1) * SCORE_SCALE
        return (holding.astype(F32) - LR_EMBED * held_grad).astype(BF16)

    def left_update(table, grad):
        row_grad = dot(rel_ref[...], grad, 1, 0)
        high = row_grad.astype(BF16)
        low = (row_grad - high.astype(F32)).astype(BF16)
        hot = onehot[...]
        left_grad = dot(hot, high, 1, 1) + dot(hot, low, 1, 1)
        return (table.astype(F32) - LR_EMBED * left_grad).astype(BF16)

    def relation_grad(grad):
        return dot(picked[...], grad, 1, 1)

    make_queries(0, left_ref[...])
    for copy in move0:
        copy.wait()
    make_coeffs(met0[...], query[0], meta[0:1, :])
    grad = query_grad(met0[...])
    total = relation_grad(grad)
    left_out[...] = left_update(left_ref[...], grad)
    make_queries(1, left_out[...])
    ask1 = remote(query.at[1], query_in1, small_send.at[2], small_recv.at[2], inner_id(second))
    ask1.start()
    for i in range(ROW_CHUNKS):
        met1[piece(i), :] = held_update(met0[piece(i), :], query[0], i)

    meta1.wait()
    ask1.wait()
    make_coeffs(met1[...], query_in1[...], meta_in1[1:2, :])
    move2 = [
        remote(met2.at[piece(i)], own2.at[piece(i)], move2_send.at[i], move2_recv.at[i], inner_id(third))
        for i in range(ROW_CHUNKS)
    ]
    grad_out1[...] = query_grad(met1[...])
    back1 = remote(grad_out1, grad_in1, small_send.at[3], small_recv.at[3], inner_id(second))
    back1.start()
    for i in range(ROW_CHUNKS):
        met2[piece(i), :] = held_update(met1[piece(i), :], query_in1[...], i)
        move2[i].start()
    back1.wait()
    grad = grad_in1[...]
    total = total + relation_grad(grad)
    left_out[...] = left_update(left_out[...], grad)

    make_queries(2, left_out[...])
    ask2 = remote(query.at[2], query_in2, small_send.at[4], small_recv.at[4], inner_id(fourth))
    ask2.start()
    move3 = [
        remote(own2.at[piece(i)], next3.at[piece(i)], move3_send.at[i], move3_recv.at[i], inner_id(fourth))
        for i in range(ROW_CHUNKS)
    ]
    for i in range(ROW_CHUNKS):
        move2[i].wait()
        move3[i].start()
    make_coeffs(own2[...], query[2], meta[2:3, :])
    grad = query_grad(own2[...])
    total = total + relation_grad(grad)
    left_out[...] = left_update(left_out[...], grad)
    make_queries(3, left_out[...])
    meta3.wait()
    ask2.wait()
    for copy in move3:
        copy.wait()
    make_coeffs(next3[...], query_in2[...], meta_in3[2:3, :])
    for i in range(ROW_CHUNKS):
        right_out[piece(i), :] = held_update(next3[piece(i), :], query_in2[...], i)

    make_coeffs(right_out[...], query[3], meta[3:4, :])
    grad = query_grad(right_out[...])
    total = total + relation_grad(grad)

    share = rel_ref.shape[0] // n_inner
    for i in range(n_inner):
        part[i] = total[i * share : (i + 1) * share, :].astype(BF16)
    scatter = []
    for step in range(1, n_inner):
        to = lax.rem(me + step, n_inner)
        copy = remote(
            part.at[to], part_in.at[step - 1], rs_send.at[step - 1], rs_recv.at[step - 1], inner_id(to)
        )
        copy.start()
        scatter.append(copy)
    for i in range(ROW_CHUNKS):
        right_out[piece(i), :] = held_update(right_out[piece(i), :], query[3], i)
    left_out[...] = left_update(left_out[...], grad)
    own = part[me].astype(F32)
    for step, copy in enumerate(scatter):
        copy.wait()
        own = own + part_in[step].astype(F32)
    shard[...] = own
    everyone = []
    for step in range(1, n_group):
        to = lax.rem(my_group + step, n_group)
        copy = remote(
            shard, shard_in.at[my_group], ar_send.at[step - 1], ar_recv.at[step - 1], group_id(to)
        )
        copy.start()
        everyone.append(copy)
    shard_in[my_group] = own
    for copy in everyone:
        copy.wait()
    whole = shard_in[0]
    for g in range(1, n_group):
        whole = whole + shard_in[g]
    gathered[me] = whole.astype(BF16)
    spread = []
    for step in range(1, n_inner):
        to = lax.rem(me + step, n_inner)
        copy = remote(
            gathered.at[me], gathered.at[me], ag_send.at[step - 1], ag_recv.at[step - 1], inner_id(to)
        )
        copy.start()
        spread.append(copy)
    for copy in spread:
        copy.wait()
    for i in range(n_inner):
        here = slice(i * share, (i + 1) * share)
        rel_out[here, :] = rel_ref[here, :].astype(F32) - LR_RELATION * gathered[i].astype(F32)


def shards(left_part, right_part, relation, src_index, dst_index, lengths):
    n_inner = lax.axis_size("inner")
    n_group = lax.axis_size("group")
    rows, depth = left_part.shape
    slots = src_index.shape[2]
    share = depth // n_inner
    block = pltpu.VMEM((rows, depth), BF16)
    asked = pltpu.VMEM((depth, slots), BF16)
    meta = pltpu.VMEM((2 * MEETINGS, slots), jnp.int32)
    dma = pltpu.SemaphoreType.DMA
    vmem = pl.BlockSpec(memory_space=pltpu.VMEM)

    def body(*refs):
        kernel(n_inner, n_group, *refs)

    return pl.pallas_call(
        body,
        out_shape=(
            jax.ShapeDtypeStruct((rows, depth), BF16),
            jax.ShapeDtypeStruct((rows, depth), BF16),
            jax.ShapeDtypeStruct((depth, depth), F32),
        ),
        in_specs=[vmem] * 6,
        out_specs=(vmem,) * 3,
        scratch_shapes=[
            block,
            block,
            block,
            block,
            block,
            asked,
            pltpu.VMEM((MEETINGS, depth, slots), BF16),
            asked,
            asked,
            asked,
            asked,
            pltpu.VMEM((rows, slots), BF16),
            pltpu.VMEM((rows, slots), BF16),
            meta,
            meta,
            meta,
            pltpu.VMEM((n_inner, share, depth), BF16),
            pltpu.VMEM((n_inner - 1, share, depth), BF16),
            pltpu.VMEM((share, depth), F32),
            pltpu.VMEM((n_group, share, depth), F32),
            pltpu.VMEM((n_inner, share, depth), BF16),
            dma((ROW_CHUNKS,)),
            dma((ROW_CHUNKS,)),
            dma((ROW_CHUNKS,)),
            dma((ROW_CHUNKS,)),
            dma((ROW_CHUNKS,)),
            dma((ROW_CHUNKS,)),
            dma((5,)),
            dma((5,)),
            dma((n_inner - 1,)),
            dma((n_inner - 1,)),
            dma((n_group - 1,)),
            dma((n_group - 1,)),
            dma((n_inner - 1,)),
            dma((n_inner - 1,)),
        ],
        compiler_params=pltpu.CompilerParams(
            collective_id=0, has_side_effects=True, vmem_limit_bytes=48 * 1024 * 1024
        ),
        cost_estimate=pl.CostEstimate(
            flops=MEETINGS * 12 * rows * slots * depth,
            bytes_accessed=8 * rows * depth,
            transcendentals=MEETINGS * rows * slots,
        ),
        name="bucket_meetings",
    )(left_part, right_part, relation, src_index, dst_index, lengths)


def solution(mesh):
    in_specs = (
        P(("group", "inner"), None),
        P(("group", "inner"), None),
        P(),
        P(("group", "inner"), None, None),
        P(("group", "inner"), None, None),
        P(("group", "inner"), None),
    )
    out_specs = (P(("group", "inner"), None), P(("group", "inner"), None), P())
    return jax.shard_map(shards, mesh=mesh, in_specs=in_specs, out_specs=out_specs, check_vma=False)
```

time: 220 us -> 84.2 us (0.38)
  waiting for transfers between devices: 164 us -> 0 us
  Pallas kernels: 0 us -> 75.9 us
  matrix products: 20 us -> 0 us
  between operations: 14.3 us -> 0.66 us
  other arithmetic: 9.83 us -> 0 us
  starting transfers between devices: 8.7 us -> 0 us
  local copies, waits for them, and re-layouts: 3.2 us -> 7.32 us
    psum x1 -> x0, waiting for transfers between devices: 124 us -> none  [shards(): grad_total = grad_total + lax.psum(relation_grad, ('group', 'inner'))]
    pallas_call x0 -> x1, Pallas kernels: none -> 75.9 us  [shards(): pl.pallas_call(body, out_shape=(jax.ShapeDtypeStruct((rows, depth), BF16)...]
    ppermute x4 -> x0, waiting for transfers between devices: 39.9 us -> none  [swapped(): return lax.ppermute(value, axis, pairs)]
    dot_general x32 -> x0, matrix products: 20 us -> none  [the longest x4 3.37 us: bucket(): lax.dot_general(summed_rows, relation.astype(jnp.float32), (((1,), (1,)),...]
    ppermute x4 -> x0, starting transfers between devices: 8.66 us -> none  [swapped(): return lax.ppermute(value, axis, pairs)]
    unnamed x4 -> x15, local copies, waits for them, and re-layouts: 0.01 us -> 7.32 us
    convert_element_type x8 -> x0, other arithmetic: 6.04 us -> none  [the longest x4 3.4 us: bucket(): coeffs = ((softmax_w - target) * live_mask[:, None]).astype(jnp.bfloat16)]
    slice x3 -> x0, local copies, waits for them, and re-layouts: 3.18 us -> none  [the longest x1 1.47 us: shards(): lengths[0, meeting]]
  transfers between devices with their start and end apart: 5 -> 0, of which waited for: 5 -> 0; matrix products, arithmetic and copies ran while one was open for 9% -> 0% of each run, Pallas kernels for 0% -> 0%
where the time goes in v1:
time: 84.2 us; the launch traced here: 83.9 us
  Pallas kernels  75.9 us (90%)
  local copies, waits for them, and re-layouts  7.32 us (9%)
    pallas_call x1, Pallas kernels, shards(): pl.pallas_call(body, out_shape=(jax.ShapeDtypeStruct((rows, depth), BF16)...  75.9 us
    unnamed x15, local copies, waits for them, and re-layouts  7.32 us

profile of v1, /device:TPU:0, one launch (start us, length us, event | category | flops | bytes accessed | tf_op | source)
XLA Modules:
  0.0 83.9 jit_solution(9537843740547450188)
XLA Ops:
  0.6 0.0 copy-start
  0.6 1.0 %copy-done = bf16[1024,256]{1,0:T(8,128)(2,1)S(1)} copy-done((bf16[1024,256]{1,0:T(8,128)(2,1)S(1)}, bf16[1024,256]{1,0:T(8,128)(2,1)}, u32[]{:S(2)}) %copy-start) | copy-done | bytes 524312
  1.7 0.0 copy-start.1
  1.7 1.0 %copy-done.1 = bf16[1024,256]{1,0:T(8,128)(2,1)S(1)} copy-done((bf16[1024,256]{1,0:T(8,128)(2,1)S(1)}, bf16[1024,256]{1,0:T(8,128)(2,1)}, u32[]{:S(2)}) %copy-start.1) | copy-done | bytes 524312
  2.7 0.0 copy-start.2
  2.7 0.9 %copy-done.2 = bf16[256,256]{1,0:T(8,128)(2,1)S(1)} copy-done((bf16[256,256]{1,0:T(8,128)(2,1)S(1)}, bf16[256,256]{1,0:T(8,128)(2,1)}, u32[]{:S(2)}) %copy-start.2) | copy-done | bytes 131096
  3.6 0.0 copy-start.3
  3.6 0.7 copy-done.3
  4.3 0.0 copy-start.4
  4.3 0.7 copy-done.4
  5.0 0.0 copy-start.5
  5.0 0.7 copy-done.5
  5.7 75.9 %bucket_meetings.1 = (bf16[1024,256]{1,0:T(8,128)(2,1)S(1)}, bf16[1024,256]{1,0:T(8,128)(2,1)S(1)}, f32[256,256]{1,0:T(8,128)S(1)}) custom-call(bf16[1024,256]{1,0:T(8,128)(2,1)S(1)} %copy-done, bf16[1024,256]{1,0:T(8,128)(2,1)S(1)} %copy-done.1, bf16[256,256]{1,0:T(8,128)(2,1)S(1)} %copy-done.2, s32[1,4,512]{2,1,0:T(4,128)S(1)} %copy-done.3, ...), custom_call_target="tpu_custom_call" | custom-call | flops 6442450944 | bytes 2097152 | tf_op jit(solution)/shard_map/bucket_meetings/pallas_call | solution.py:295
  81.6 0.8 copy.12
  82.4 0.8 copy.13
  83.2 0.7 copy.14
Async XLA Ops:
  0.6 1.0 %copy-start = (bf16[1024,256]{1,0:T(8,128)(2,1)S(1)}, bf16[1024,256]{1,0:T(8,128)(2,1)}, u32[]{:S(2)}) copy-start(bf16[1024,256]{1,0:T(8,128)(2,1)} %refs_0_.1) | copy-start | bytes 1572868
  1.7 1.0 %copy-start.1 = (bf16[1024,256]{1,0:T(8,128)(2,1)S(1)}, bf16[1024,256]{1,0:T(8,128)(2,1)}, u32[]{:S(2)}) copy-start(bf16[1024,256]{1,0:T(8,128)(2,1)} %refs_1_.1) | copy-start | bytes 1572868
  2.7 0.9 %copy-start.2 = (bf16[256,256]{1,0:T(8,128)(2,1)S(1)}, bf16[256,256]{1,0:T(8,128)(2,1)}, u32[]{:S(2)}) copy-start(bf16[256,256]{1,0:T(8,128)(2,1)} %refs_2_.1) | copy-start | bytes 393220
  3.6 0.7 copy-start.3
  4.3 0.7 copy-start.4
  5.0 0.7 copy-start.5

commit v2 on v1

--- a/solution.py
+++ b/solution.py
@@ -36,9 +36,11 @@
     src_ref,
     dst_ref,
     len_ref,
+    left_final,
+    right_final,
+    rel_out,
     left_out,
     right_out,
-    rel_out,
     met0,
     met1,
     met2,
@@ -48,10 +50,13 @@
     query,
     query_in1,
     query_in2,
-    grad_out1,
-    grad_in1,
+    grads,
     coeffs,
+    expo,
     onehot,
+    rel_own,
+    src_own,
+    dst_own,
     meta,
     meta_in1,
     meta_in3,
@@ -68,6 +73,10 @@
     move3_recv,
     small_send,
     small_recv,
+    ask1_send,
+    ask1_recv,
+    load,
+    store,
     rs_send,
     rs_recv,
     ar_send,
@@ -102,6 +111,15 @@
     def piece(i):
         return pl.ds(i * chunk, chunk)
 
+    loads = [
+        pltpu.make_async_copy(src, dst, load.at[i])
+        for i, (src, dst) in enumerate(
+            [(dst_ref, dst_own), (src_ref, src_own), (left_ref, left_out), (rel_ref, rel_own)]
+        )
+    ]
+    for copy in loads:
+        copy.start()
+
     barrier = pltpu.get_barrier_semaphore()
     for step in range(1, n_inner):
         pl.semaphore_signal(
@@ -120,113 +138,151 @@
     for copy in move0:
         copy.start()
 
+    for copy in loads:
+        copy.wait()
+
     slot_ids = lax.broadcasted_iota(jnp.int32, (1, slots), 1)
     meta[...] = jnp.zeros_like(meta)
     for m in range(MEETINGS):
-        meta[m : m + 1, :] = jnp.where(slot_ids < len_ref[0:1, m : m + 1], dst_ref[0, m : m + 1, :], -1)
+        meta[m : m + 1, :] = jnp.where(slot_ids < len_ref[0:1, m : m + 1], dst_own[0, m : m + 1, :], -1)
     meta1 = remote(meta, meta_in1, small_send.at[0], small_recv.at[0], inner_id(second))
     meta3 = remote(meta, meta_in3, small_send.at[1], small_recv.at[1], inner_id(fourth))
     meta1.start()
     meta3.start()
 
-    entity = lax.broadcasted_iota(jnp.int32, (rows, width), 0)
-
-    def columns(i):
-        return slice(i * width, (i + 1) * width)
-
-    def make_queries(m, table):
-        for i in range(EDGE_CHUNKS):
-            hot = (entity == src_ref[0, m : m + 1, columns(i)]).astype(F32).astype(BF16)
-            onehot[:, columns(i)] = hot
-            chosen = dot(table, hot, 0, 0).astype(BF16)
-            picked[:, columns(i)] = chosen
-            query[m, :, columns(i)] = dot(rel_ref[...], chosen, 0, 0).astype(BF16)
-
-    def make_coeffs(holding, asked, targets):
-        for i in range(EDGE_CHUNKS):
-            scores = dot(holding, asked[:, columns(i)], 1, 0) * SCORE_SCALE
-            expos = jnp.exp(scores - jnp.max(scores, axis=0, keepdims=True))
-            weight = expos * (1.0 / jnp.sum(expos, axis=0, keepdims=True))
-            target = targets[:, columns(i)]
-            weight = weight - (entity == target).astype(F32)
-            weight = weight * (target >= 0).astype(F32)
-            coeffs[:, columns(i)] = weight.astype(BF16)
-
-    def query_grad(holding):
-        return (dot(holding, coeffs[...], 0, 0) * SCORE_SCALE).astype(BF16)
+    entity = lax.broadcasted_iota(jnp.int32, (chunk, slots), 0)
+    every = slice(0, slots)
+    halves = [slice(i * width, (i + 1) * width) for i in range(EDGE_CHUNKS)]
+
+    def make_onehot(m):
+        for i in range(ROW_CHUNKS):
+            hot = entity == src_own[0, m : m + 1, :] - i * chunk
+            onehot[m, piece(i), :] = hot.astype(F32).astype(BF16)
+
+    def make_queries(m, cols):
+        chosen = dot(left_out[...], onehot[m, :, cols], 0, 0).astype(BF16)
+        picked[m, :, cols] = chosen
+        query[m, :, cols] = dot(rel_own[...], chosen, 0, 0).astype(BF16)
+
+    def score_piece(holding, asked, buffer, i, cols):
+        scores = dot(holding, asked, 1, 0) * SCORE_SCALE
+        top = jnp.max(scores, axis=0, keepdims=True)
+        expos = jnp.exp(scores - top)
+        expo[buffer, piece(i), cols] = expos
+        return top, jnp.sum(expos, axis=0, keepdims=True)
+
+    def finish_coeffs(stats, targets, buffer, cols):
+        top = stats[0][0]
+        for piece_top, _ in stats[1:]:
+            top = jnp.maximum(top, piece_top)
+        factors = [jnp.exp(piece_top - top) for piece_top, _ in stats]
+        whole = sum(factor * piece_sum for factor, (_, piece_sum) in zip(factors, stats))
+        inverse = (targets >= 0).astype(F32) / whole
+        for i, factor in enumerate(factors):
+            weight = expo[buffer, piece(i), cols] * (factor * inverse)
+            hit = entity[:, cols] == targets - i * chunk
+            coeffs[piece(i), cols] = jnp.where(hit, weight - 1.0, weight).astype(BF16)
+
+    def make_grad(m, holding):
+        grads[m] = (dot(holding, coeffs[...], 0, 0) * SCORE_SCALE).astype(BF16)
 
     def held_update(holding, asked, i):
         held_grad = dot(coeffs[piece(i), :], asked, 1, 1) * SCORE_SCALE
         return (holding.astype(F32) - LR_EMBED * held_grad).astype(BF16)
 
-    def left_update(table, grad):
-        row_grad = dot(rel_ref[...], grad, 1, 0)
-        high = row_grad.astype(BF16)
-        low = (row_grad - high.astype(F32)).astype(BF16)
-        hot = onehot[...]
-        left_grad = dot(hot, high, 1, 1) + dot(hot, low, 1, 1)
-        return (table.astype(F32) - LR_EMBED * left_grad).astype(BF16)
-
-    def relation_grad(grad):
-        return dot(picked[...], grad, 1, 1)
-
-    make_queries(0, left_ref[...])
-    for copy in move0:
-        copy.wait()
-    make_coeffs(met0[...], query[0], meta[0:1, :])
-    grad = query_grad(met0[...])
-    total = relation_grad(grad)
-    left_out[...] = left_update(left_ref[...], grad)
-    make_queries(1, left_out[...])
-    ask1 = remote(query.at[1], query_in1, small_send.at[2], small_recv.at[2], inner_id(second))
-    ask1.start()
+    def left_update(m):
+        row_grad = dot(rel_own[...], grads[m], 1, 0).astype(BF16)
+        for i in range(ROW_CHUNKS):
+            left_grad = dot(onehot[m, piece(i), :], row_grad, 1, 1)
+            left_out[piece(i), :] = (left_out[piece(i), :].astype(F32) - LR_EMBED * left_grad).astype(BF16)
+
+    def relation_grad(m):
+        return dot(picked[m], grads[m], 1, 1)
+
+    make_onehot(0)
+    make_queries(0, every)
+    for m in range(1, MEETINGS):
+        make_onehot(m)
+    stats = []
+    for i in range(ROW_CHUNKS):
+        move0[i].wait()
+        stats.append(score_piece(met0[piece(i), :], query[0], 0, i, every))
+    finish_coeffs(stats, meta[0:1, :], 0, every)
+    make_grad(0, met0[...])
+    left_update(0)
+    ask1 = [
+        remote(
+            query.at[1, :, cols], query_in1.at[:, cols], ask1_send.at[i], ask1_recv.at[i], inner_id(second)
+        )
+        for i, cols in enumerate(halves)
+    ]
+    for i, cols in enumerate(halves):
+        make_queries(1, cols)
+        ask1[i].start()
     for i in range(ROW_CHUNKS):
         met1[piece(i), :] = held_update(met0[piece(i), :], query[0], i)
+    total = relation_grad(0)
 
     meta1.wait()
-    ask1.wait()
-    make_coeffs(met1[...], query_in1[...], meta_in1[1:2, :])
+    for half, cols in enumerate(halves):
+        ask1[half].wait()
+        stats = [
+            score_piece(met1[piece(i), :], query_in1[:, cols], 0, i, cols) for i in range(ROW_CHUNKS)
+        ]
+        finish_coeffs(stats, meta_in1[1:2, cols], 0, cols)
     move2 = [
         remote(met2.at[piece(i)], own2.at[piece(i)], move2_send.at[i], move2_recv.at[i], inner_id(third))
         for i in range(ROW_CHUNKS)
     ]
-    grad_out1[...] = query_grad(met1[...])
-    back1 = remote(grad_out1, grad_in1, small_send.at[3], small_recv.at[3], inner_id(second))
-    back1.start()
-    for i in range(ROW_CHUNKS):
+    back1 = remote(grads.at[MEETINGS], grads.at[1], small_send.at[3], small_recv.at[3], inner_id(second))
+    for i in range(ROW_CHUNKS):
+        if i == ROW_CHUNKS // 2:
+            make_grad(MEETINGS, met1[...])
+            back1.start()
         met2[piece(i), :] = held_update(met1[piece(i), :], query_in1[...], i)
         move2[i].start()
     back1.wait()
-    grad = grad_in1[...]
-    total = total + relation_grad(grad)
-    left_out[...] = left_update(left_out[...], grad)
-
-    make_queries(2, left_out[...])
+    left_update(1)
+
+    make_queries(2, every)
     ask2 = remote(query.at[2], query_in2, small_send.at[4], small_recv.at[4], inner_id(fourth))
     ask2.start()
+    total = total + relation_grad(1)
     move3 = [
         remote(own2.at[piece(i)], next3.at[piece(i)], move3_send.at[i], move3_recv.at[i], inner_id(fourth))
         for i in range(ROW_CHUNKS)
     ]
+    stats = []
+    next_stats = []
+
+    def score_next(i):
+        move3[i].wait()
+        next_stats.append(score_piece(next3[piece(i), :], query_in2[...], 1, i, every))
+
     for i in range(ROW_CHUNKS):
         move2[i].wait()
         move3[i].start()
-    make_coeffs(own2[...], query[2], meta[2:3, :])
-    grad = query_grad(own2[...])
-    total = total + relation_grad(grad)
-    left_out[...] = left_update(left_out[...], grad)
-    make_queries(3, left_out[...])
-    meta3.wait()
-    ask2.wait()
-    for copy in move3:
-        copy.wait()
-    make_coeffs(next3[...], query_in2[...], meta_in3[2:3, :])
+        stats.append(score_piece(own2[piece(i), :], query[2], 0, i, every))
+        if i == 1:
+            meta3.wait()
+            ask2.wait()
+        if i > 0:
+            score_next(i - 1)
+    finish_coeffs(stats, meta[2:3, :], 0, every)
+    make_grad(2, own2[...])
+    left_update(2)
+    make_queries(3, every)
+    total = total + relation_grad(2)
+    score_next(ROW_CHUNKS - 1)
+    finish_coeffs(next_stats, meta_in3[2:3, :], 1, every)
+
+    stats = []
     for i in range(ROW_CHUNKS):
         right_out[piece(i), :] = held_update(next3[piece(i), :], query_in2[...], i)
-
-    make_coeffs(right_out[...], query[3], meta[3:4, :])
-    grad = query_grad(right_out[...])
-    total = total + relation_grad(grad)
+        stats.append(score_piece(right_out[piece(i), :], query[3], 0, i, every))
+    finish_coeffs(stats, meta[3:4, :], 0, every)
+    make_grad(3, right_out[...])
+    total = total + relation_grad(3)
 
     share = rel_ref.shape[0] // n_inner
     for i in range(n_inner):
@@ -241,7 +297,13 @@
         scatter.append(copy)
     for i in range(ROW_CHUNKS):
         right_out[piece(i), :] = held_update(right_out[piece(i), :], query[3], i)
-    left_out[...] = left_update(left_out[...], grad)
+    left_update(3)
+    stores = [
+        pltpu.make_async_copy(right_out, right_final, store.at[0]),
+        pltpu.make_async_copy(left_out, left_final, store.at[1]),
+    ]
+    for copy in stores:
+        copy.start()
     own = part[me].astype(F32)
     for step, copy in enumerate(scatter):
         copy.wait()
@@ -274,7 +336,9 @@
         copy.wait()
     for i in range(n_inner):
         here = slice(i * share, (i + 1) * share)
-        rel_out[here, :] = rel_ref[here, :].astype(F32) - LR_RELATION * gathered[i].astype(F32)
+        rel_out[here, :] = rel_own[here, :].astype(F32) - LR_RELATION * gathered[i].astype(F32)
+    for copy in stores:
+        copy.wait()
 
 
 def shards(left_part, right_part, relation, src_index, dst_index, lengths):
@@ -288,6 +352,7 @@
     meta = pltpu.VMEM((2 * MEETINGS, slots), jnp.int32)
     dma = pltpu.SemaphoreType.DMA
     vmem = pl.BlockSpec(memory_space=pltpu.VMEM)
+    hbm = pl.BlockSpec(memory_space=pltpu.HBM)
 
     def body(*refs):
         kernel(n_inner, n_group, *refs)
@@ -299,22 +364,27 @@
             jax.ShapeDtypeStruct((rows, depth), BF16),
             jax.ShapeDtypeStruct((depth, depth), F32),
         ),
-        in_specs=[vmem] * 6,
-        out_specs=(vmem,) * 3,
+        in_specs=[hbm] * 5 + [vmem],
+        out_specs=(hbm, hbm, vmem),
         scratch_shapes=[
             block,
             block,
             block,
             block,
             block,
-            asked,
+            block,
+            block,
+            pltpu.VMEM((MEETINGS, depth, slots), BF16),
             pltpu.VMEM((MEETINGS, depth, slots), BF16),
             asked,
             asked,
-            asked,
-            asked,
+            pltpu.VMEM((MEETINGS + 1, depth, slots), BF16),
             pltpu.VMEM((rows, slots), BF16),
-            pltpu.VMEM((rows, slots), BF16),
+            pltpu.VMEM((2, rows, slots), F32),
+            pltpu.VMEM((MEETINGS, rows, slots), BF16),
+            pltpu.VMEM(relation.shape, BF16),
+            pltpu.VMEM(src_index.shape, jnp.int32),
+            pltpu.VMEM(dst_index.shape, jnp.int32),
             meta,
             meta,
             meta,
@@ -331,6 +401,10 @@
             dma((ROW_CHUNKS,)),
             dma((5,)),
             dma((5,)),
+            dma((EDGE_CHUNKS,)),
+            dma((EDGE_CHUNKS,)),
+            dma((4,)),
+            dma((2,)),
             dma((n_inner - 1,)),
             dma((n_inner - 1,)),
             dma((n_group - 1,)),
@@ -339,7 +413,7 @@
             dma((n_inner - 1,)),
         ],
         compiler_params=pltpu.CompilerParams(
-            collective_id=0, has_side_effects=True, vmem_limit_bytes=48 * 1024 * 1024
+            collective_id=0, has_side_effects=True, vmem_limit_bytes=64 * 1024 * 1024 - 512 * 1024
         ),
         cost_estimate=pl.CostEstimate(
             flops=MEETINGS * 12 * rows * slots * depth,

time: 84.2 us -> 83.8 us (level)
  local copies, waits for them, and re-layouts: 7.32 us -> 3.72 us
  Pallas kernels: 75.9 us -> 79.2 us
    unnamed x15 -> x7, local copies, waits for them, and re-layouts: 7.32 us -> 3.72 us
    pallas_call x1, Pallas kernels: 75.9 us -> 79.2 us  [shards(): pl.pallas_call(body, out_shape=(jax.ShapeDtypeStruct((rows, depth), BF16)...]
where the time goes in v2:
time: 83.8 us; the launch traced here: 83.6 us
  Pallas kernels  79.2 us (95%)
  local copies, waits for them, and re-layouts  3.72 us (4%)
    pallas_call x1, Pallas kernels, shards(): pl.pallas_call(body, out_shape=(jax.ShapeDtypeStruct((rows, depth), BF16)...  79.2 us
    unnamed x7, local copies, waits for them, and re-layouts  3.72 us

profile of v2, /device:TPU:0, one launch (start us, length us, event | category | flops | bytes accessed | tf_op | source)
XLA Modules:
  0.0 83.6 jit_solution(4372304310175991534)
XLA Ops:
  0.6 79.2 %bucket_meetings.1 = (bf16[1024,256]{1,0:T(8,128)(2,1)}, bf16[1024,256]{1,0:T(8,128)(2,1)}, f32[256,256]{1,0:T(8,128)}) custom-call(bf16[1024,256]{1,0:T(8,128)(2,1)} %refs_0_.1, bf16[1024,256]{1,0:T(8,128)(2,1)} %refs_1_.1, bf16[256,256]{1,0:T(8,128)(2,1)} %refs_2_.1, s32[1,4,512]{2,1,0:T(4,128)} %refs_3_.1, s32[1,4,512]{2,1,0:T(4,128)} %refs_4_.1, ...), custom_call_target="tpu_custom_call" | custom-call | flops 6442450944 | bytes 2097152 | tf_op jit(solution)/shard_map/bucket_meetings/pallas_call | solution.py:360
  79.8 0.0 copy-start
  79.9 1.9 %copy.12 = bf16[1024,256]{1,0:T(8,128)(2,1)} copy(bf16[1024,256]{1,0:T(8,128)(2,1)} %get-tuple-element.6) | data formatting | bytes 1048576
  81.8 0.0 copy-done
  81.8 0.0 copy-start.1
  81.8 0.8 copy.13
  82.6 0.3 copy-done.1
  82.9 0.7 copy.14
Async XLA Ops:
  79.8 1.9 %copy-start = (bf16[1024,256]{1,0:T(8,128)(2,1)S(1)}, bf16[1024,256]{1,0:T(8,128)(2,1)}, u32[]{:S(2)}) copy-start(bf16[1024,256]{1,0:T(8,128)(2,1)} %get-tuple-element.7) | copy-start | bytes 1572868
  81.8 1.1 %copy-start.1 = (f32[256,256]{1,0:T(8,128)S(1)}, f32[256,256]{1,0:T(8,128)}, u32[]{:S(2)}) copy-start(f32[256,256]{1,0:T(8,128)} %get-tuple-element.8) | copy-start | bytes 786436

commit v3 on v2

--- a/solution.py
+++ b/solution.py
@@ -16,7 +16,7 @@
 BF16 = jnp.bfloat16
 
 ROW_CHUNKS = 4
-EDGE_CHUNKS = 2
+VMEM_LIMIT = 64 * 1024 * 1024 - 512 * 1024
 
 
 def partner(index, mask):
@@ -42,6 +42,7 @@
     left_out,
     right_out,
     met0,
+    next1,
     met1,
     met2,
     own2,
@@ -73,8 +74,8 @@
     move3_recv,
     small_send,
     small_recv,
-    ask1_send,
-    ask1_recv,
+    move1_send,
+    move1_recv,
     load,
     store,
     rs_send,
@@ -92,10 +93,9 @@
     masks = [2 ** (m % log_inner) for m in range(MEETINGS)]
     first = partner(me, masks[0])
     second = partner(me, masks[1])
-    third = partner(second, masks[2])
+    third = partner(me, masks[2])
     fourth = partner(me, masks[3])
     chunk = rows // ROW_CHUNKS
-    width = slots // EDGE_CHUNKS
 
     def inner_id(index):
         return (my_group, index)
@@ -152,7 +152,6 @@
 
     entity = lax.broadcasted_iota(jnp.int32, (chunk, slots), 0)
     every = slice(0, slots)
-    halves = [slice(i * width, (i + 1) * width) for i in range(EDGE_CHUNKS)]
 
     def make_onehot(m):
         for i in range(ROW_CHUNKS):
@@ -199,88 +198,66 @@
     def relation_grad(m):
         return dot(picked[m], grads[m], 1, 1)
 
+    def paired(m, moves, passes, ask, own, after, asked, notice, their_targets, result):
+        stats, after_stats = [], []
+
+        def score_after(i):
+            passes[i].wait()
+            after_stats.append(score_piece(after[piece(i), :], asked[...], 1, i, every))
+
+        for i in range(ROW_CHUNKS):
+            moves[i].wait()
+            passes[i].start()
+            stats.append(score_piece(own[piece(i), :], query[m], 0, i, every))
+            if i == 1:
+                notice.wait()
+                ask.wait()
+            if i > 0:
+                score_after(i - 1)
+        finish_coeffs(stats, meta[m : m + 1, :], 0, every)
+        make_grad(m, own[...])
+        left_update(m)
+        make_queries(m + 1, every)
+        grad_sum = relation_grad(m)
+        score_after(ROW_CHUNKS - 1)
+        finish_coeffs(after_stats, their_targets[m : m + 1, :], 1, every)
+        stats = []
+        for i in range(ROW_CHUNKS):
+            result[piece(i), :] = held_update(after[piece(i), :], asked[...], i)
+            stats.append(score_piece(result[piece(i), :], query[m + 1], 0, i, every))
+        finish_coeffs(stats, meta[m + 1 : m + 2, :], 0, every)
+        return grad_sum
+
     make_onehot(0)
     make_queries(0, every)
+    ask0 = remote(query.at[0], query_in1, small_send.at[2], small_recv.at[2], inner_id(second))
+    ask0.start()
     for m in range(1, MEETINGS):
         make_onehot(m)
-    stats = []
-    for i in range(ROW_CHUNKS):
-        move0[i].wait()
-        stats.append(score_piece(met0[piece(i), :], query[0], 0, i, every))
-    finish_coeffs(stats, meta[0:1, :], 0, every)
-    make_grad(0, met0[...])
-    left_update(0)
-    ask1 = [
-        remote(
-            query.at[1, :, cols], query_in1.at[:, cols], ask1_send.at[i], ask1_recv.at[i], inner_id(second)
-        )
-        for i, cols in enumerate(halves)
-    ]
-    for i, cols in enumerate(halves):
-        make_queries(1, cols)
-        ask1[i].start()
-    for i in range(ROW_CHUNKS):
-        met1[piece(i), :] = held_update(met0[piece(i), :], query[0], i)
-    total = relation_grad(0)
-
-    meta1.wait()
-    for half, cols in enumerate(halves):
-        ask1[half].wait()
-        stats = [
-            score_piece(met1[piece(i), :], query_in1[:, cols], 0, i, cols) for i in range(ROW_CHUNKS)
-        ]
-        finish_coeffs(stats, meta_in1[1:2, cols], 0, cols)
+    move1 = [
+        remote(met0.at[piece(i)], next1.at[piece(i)], move1_send.at[i], move1_recv.at[i], inner_id(second))
+        for i in range(ROW_CHUNKS)
+    ]
+    total = paired(0, move0, move1, ask0, met0, next1, query_in1, meta1, meta_in1, met1)
     move2 = [
         remote(met2.at[piece(i)], own2.at[piece(i)], move2_send.at[i], move2_recv.at[i], inner_id(third))
         for i in range(ROW_CHUNKS)
     ]
-    back1 = remote(grads.at[MEETINGS], grads.at[1], small_send.at[3], small_recv.at[3], inner_id(second))
     for i in range(ROW_CHUNKS):
-        if i == ROW_CHUNKS // 2:
-            make_grad(MEETINGS, met1[...])
-            back1.start()
-        met2[piece(i), :] = held_update(met1[piece(i), :], query_in1[...], i)
+        met2[piece(i), :] = held_update(met1[piece(i), :], query[1], i)
         move2[i].start()
-    back1.wait()
+    make_grad(1, met1[...])
     left_update(1)
 
     make_queries(2, every)
-    ask2 = remote(query.at[2], query_in2, small_send.at[4], small_recv.at[4], inner_id(fourth))
+    ask2 = remote(query.at[2], query_in2, small_send.at[3], small_recv.at[3], inner_id(fourth))
     ask2.start()
     total = total + relation_grad(1)
     move3 = [
         remote(own2.at[piece(i)], next3.at[piece(i)], move3_send.at[i], move3_recv.at[i], inner_id(fourth))
         for i in range(ROW_CHUNKS)
     ]
-    stats = []
-    next_stats = []
-
-    def score_next(i):
-        move3[i].wait()
-        next_stats.append(score_piece(next3[piece(i), :], query_in2[...], 1, i, every))
-
-    for i in range(ROW_CHUNKS):
-        move2[i].wait()
-        move3[i].start()
-        stats.append(score_piece(own2[piece(i), :], query[2], 0, i, every))
-        if i == 1:
-            meta3.wait()
-            ask2.wait()
-        if i > 0:
-            score_next(i - 1)
-    finish_coeffs(stats, meta[2:3, :], 0, every)
-    make_grad(2, own2[...])
-    left_update(2)
-    make_queries(3, every)
-    total = total + relation_grad(2)
-    score_next(ROW_CHUNKS - 1)
-    finish_coeffs(next_stats, meta_in3[2:3, :], 1, every)
-
-    stats = []
-    for i in range(ROW_CHUNKS):
-        right_out[piece(i), :] = held_update(next3[piece(i), :], query_in2[...], i)
-        stats.append(score_piece(right_out[piece(i), :], query[3], 0, i, every))
-    finish_coeffs(stats, meta[3:4, :], 0, every)
+    total = total + paired(2, move2, move3, ask2, own2, next3, query_in2, meta3, meta_in3, right_out)
     make_grad(3, right_out[...])
     total = total + relation_grad(3)
 
@@ -357,7 +334,7 @@
     def body(*refs):
         kernel(n_inner, n_group, *refs)
 
-    return pl.pallas_call(
+    results = pl.pallas_call(
         body,
         out_shape=(
             jax.ShapeDtypeStruct((rows, depth), BF16),
@@ -374,11 +351,12 @@
             block,
             block,
             block,
+            block,
             pltpu.VMEM((MEETINGS, depth, slots), BF16),
             pltpu.VMEM((MEETINGS, depth, slots), BF16),
             asked,
             asked,
-            pltpu.VMEM((MEETINGS + 1, depth, slots), BF16),
+            pltpu.VMEM((MEETINGS, depth, slots), BF16),
             pltpu.VMEM((rows, slots), BF16),
             pltpu.VMEM((2, rows, slots), F32),
             pltpu.VMEM((MEETINGS, rows, slots), BF16),
@@ -399,10 +377,10 @@
             dma((ROW_CHUNKS,)),
             dma((ROW_CHUNKS,)),
             dma((ROW_CHUNKS,)),
-            dma((5,)),
-            dma((5,)),
-            dma((EDGE_CHUNKS,)),
-            dma((EDGE_CHUNKS,)),
+            dma((4,)),
+            dma((4,)),
+            dma((ROW_CHUNKS,)),
+            dma((ROW_CHUNKS,)),
             dma((4,)),
             dma((2,)),
             dma((n_inner - 1,)),
@@ -413,7 +391,7 @@
             dma((n_inner - 1,)),
         ],
         compiler_params=pltpu.CompilerParams(
-            collective_id=0, has_side_effects=True, vmem_limit_bytes=64 * 1024 * 1024 - 512 * 1024
+            collective_id=0, has_side_effects=True, vmem_limit_bytes=VMEM_LIMIT
         ),
         cost_estimate=pl.CostEstimate(
             flops=MEETINGS * 12 * rows * slots * depth,
@@ -422,6 +400,29 @@
         ),
         name="bucket_meetings",
     )(left_part, right_part, relation, src_index, dst_index, lengths)
+
+    def hand_out(*refs):
+        sems = refs[-1]
+        copies = []
+        for source, target in zip(refs[:3], refs[3:6]):
+            height = source.shape[0] // ROW_CHUNKS
+            for i in range(ROW_CHUNKS):
+                here = pl.ds(i * height, height)
+                copies.append(pltpu.make_async_copy(source.at[here], target.at[here], sems.at[len(copies)]))
+        for copy in copies:
+            copy.start()
+        for copy in copies:
+            copy.wait()
+
+    return pl.pallas_call(
+        hand_out,
+        out_shape=tuple(jax.ShapeDtypeStruct(r.shape, r.dtype) for r in results),
+        in_specs=[hbm] * 3,
+        out_specs=(hbm,) * 3,
+        scratch_shapes=[dma((3 * ROW_CHUNKS,))],
+        compiler_params=pltpu.CompilerParams(vmem_limit_bytes=VMEM_LIMIT),
+        name="hand_out",
+    )(*results)
 
 
 def solution(mesh):

time: 83.8 us -> 114 us (1.36)
  Pallas kernels: 79.2 us -> 113 us
  local copies, waits for them, and re-layouts: 3.72 us -> 0 us
    pallas_call x0 -> x1, Pallas kernels: none -> 40.9 us  [shards(): pl.pallas_call(hand_out, out_shape=tuple((jax.ShapeDtypeStruct(r.shape, r...]
    pallas_call x1, Pallas kernels: 79.2 us -> 71.9 us  [shards(): pl.pallas_call(body, out_shape=(jax.ShapeDtypeStruct((rows, depth), BF16)...]
    unnamed x7 -> x0, local copies, waits for them, and re-layouts: 3.72 us -> none
where the time goes in v3:
time: 114 us
  Pallas kernels  113 us (99%)
    pallas_call x1, Pallas kernels, shards(): pl.pallas_call(body, out_shape=(jax.ShapeDtypeStruct((rows, depth), BF16)...  71.9 us
    pallas_call x1, Pallas kernels, shards(): pl.pallas_call(hand_out, out_shape=tuple((jax.ShapeDtypeStruct(r.shape, r...  40.9 us

profile of v3, /device:TPU:0, one launch (start us, length us, event | category | flops | bytes accessed | tf_op | source)
XLA Modules:
  0.0 113.5 jit_solution(6497703066481368127)
XLA Ops:
  0.6 71.9 %bucket_meetings.1 = (bf16[1024,256]{1,0:T(8,128)(2,1)}, bf16[1024,256]{1,0:T(8,128)(2,1)}, f32[256,256]{1,0:T(8,128)}) custom-call(bf16[1024,256]{1,0:T(8,128)(2,1)} %refs_0_.1, bf16[1024,256]{1,0:T(8,128)(2,1)} %refs_1_.1, bf16[256,256]{1,0:T(8,128)(2,1)} %refs_2_.1, s32[1,4,512]{2,1,0:T(4,128)} %refs_3_.1, s32[1,4,512]{2,1,0:T(4,128)} %refs_4_.1, ...), custom_call_target="tpu_custom_call" | custom-call | flops 6442450944 | bytes 2097152 | tf_op jit(solution)/shard_map/bucket_meetings/pallas_call | solution.py:337
  72.6 40.9 %hand_out.1 = (bf16[1024,256]{1,0:T(8,128)(2,1)}, bf16[1024,256]{1,0:T(8,128)(2,1)}, f32[256,256]{1,0:T(8,128)}) custom-call(bf16[1024,256]{1,0:T(8,128)(2,1)} %get-tuple-element.6.refs_0_, bf16[1024,256]{1,0:T(8,128)(2,1)} %get-tuple-element.7.refs_1_, f32[256,256]{1,0:T(8,128)} %get-tuple-element.8.refs_2_), custom_call_target="tpu_custom_call" | custom-call | tf_op jit(solution)/shard_map/hand_out/pallas_call | solution.py:417

commit v4 on v3

--- a/solution.py
+++ b/solution.py
@@ -191,9 +191,8 @@
 
     def left_update(m):
         row_grad = dot(rel_own[...], grads[m], 1, 0).astype(BF16)
-        for i in range(ROW_CHUNKS):
-            left_grad = dot(onehot[m, piece(i), :], row_grad, 1, 1)
-            left_out[piece(i), :] = (left_out[piece(i), :].astype(F32) - LR_EMBED * left_grad).astype(BF16)
+        left_grad = dot(onehot[m], row_grad, 1, 1)
+        left_out[...] = (left_out[...].astype(F32) - LR_EMBED * left_grad).astype(BF16)
 
     def relation_grad(m):
         return dot(picked[m], grads[m], 1, 1)
@@ -402,16 +401,22 @@
     )(left_part, right_part, relation, src_index, dst_index, lengths)
 
     def hand_out(*refs):
-        sems = refs[-1]
-        copies = []
-        for source, target in zip(refs[:3], refs[3:6]):
+        sources, targets, held = refs[:3], refs[3:6], refs[6:9]
+        load, store = refs[9:]
+        loads, stores = [], []
+        for source, target, buffer in zip(sources, targets, held):
             height = source.shape[0] // ROW_CHUNKS
             for i in range(ROW_CHUNKS):
                 here = pl.ds(i * height, height)
-                copies.append(pltpu.make_async_copy(source.at[here], target.at[here], sems.at[len(copies)]))
-        for copy in copies:
+                at = len(loads)
+                loads.append(pltpu.make_async_copy(source.at[here], buffer.at[here], load.at[at]))
+                stores.append(pltpu.make_async_copy(buffer.at[here], target.at[here], store.at[at]))
+        for copy in loads:
             copy.start()
-        for copy in copies:
+        for loaded, copy in zip(loads, stores):
+            loaded.wait()
+            copy.start()
+        for copy in stores:
             copy.wait()
 
     return pl.pallas_call(
@@ -419,7 +424,7 @@
         out_shape=tuple(jax.ShapeDtypeStruct(r.shape, r.dtype) for r in results),
         in_specs=[hbm] * 3,
         out_specs=(hbm,) * 3,
-        scratch_shapes=[dma((3 * ROW_CHUNKS,))],
+        scratch_shapes=[pltpu.VMEM(r.shape, r.dtype) for r in results] + [dma((3 * ROW_CHUNKS,))] * 2,
         compiler_params=pltpu.CompilerParams(vmem_limit_bytes=VMEM_LIMIT),
         name="hand_out",
     )(*results)

time: 114 us -> 75.7 us (0.66)
  Pallas kernels: 113 us -> 74.7 us
    pallas_call x1, Pallas kernels: 40.9 us -> 2.24 us  [shards(): pl.pallas_call(hand_out, out_shape=tuple((jax.ShapeDtypeStruct(r.shape, r...]
where the time goes in v4:
time: 75.7 us; the launch traced here: 75.5 us
  Pallas kernels  74.7 us (99%)
  between operations  0.8 us (1%)
    pallas_call x1, Pallas kernels, shards(): pl.pallas_call(body, out_shape=(jax.ShapeDtypeStruct((rows, depth), BF16)...  72.5 us
    pallas_call x1, Pallas kernels, shards(): pl.pallas_call(hand_out, out_shape=tuple((jax.ShapeDtypeStruct(r.shape, r...  2.24 us

profile of v4, /device:TPU:0, one launch (start us, length us, event | category | flops | bytes accessed | tf_op | source)
XLA Modules:
  0.0 75.5 jit_solution(9531122518990560274)
XLA Ops:
  0.6 72.5 %bucket_meetings.1 = (bf16[1024,256]{1,0:T(8,128)(2,1)}, bf16[1024,256]{1,0:T(8,128)(2,1)}, f32[256,256]{1,0:T(8,128)}) custom-call(bf16[1024,256]{1,0:T(8,128)(2,1)} %refs_0_.1, bf16[1024,256]{1,0:T(8,128)(2,1)} %refs_1_.1, bf16[256,256]{1,0:T(8,128)(2,1)} %refs_2_.1, s32[1,4,512]{2,1,0:T(4,128)} %refs_3_.1, s32[1,4,512]{2,1,0:T(4,128)} %refs_4_.1, ...), custom_call_target="tpu_custom_call" | custom-call | flops 6442450944 | bytes 2097152 | tf_op jit(solution)/shard_map/bucket_meetings/pallas_call | solution.py:336
  73.1 2.2 %hand_out.1 = (bf16[1024,256]{1,0:T(8,128)(2,1)}, bf16[1024,256]{1,0:T(8,128)(2,1)}, f32[256,256]{1,0:T(8,128)}) custom-call(bf16[1024,256]{1,0:T(8,128)(2,1)} %get-tuple-element.6.refs_0_, bf16[1024,256]{1,0:T(8,128)(2,1)} %get-tuple-element.7.refs_1_, f32[256,256]{1,0:T(8,128)} %get-tuple-element.8.refs_2_), custom_call_target="tpu_custom_call" | custom-call | tf_op jit(solution)/shard_map/hand_out/pallas_call | solution.py:422
